TPU v7x, 512 devices: a whole 4x8x8 slice. The times are simulated.
512 devices in a mesh: node: 32 (over z, y_lo, core), local: 16 (over x, y_hi).
Axes of the slice: x: 4, y: 8 (y_hi: 4, y_lo: 2; y = y_hi * 2 + y_lo), z: 8, core: 2. Of those that a mesh axis runs over, the one named last changes fastest.
Arguments:
- tokens: bfloat16 [2048, 4096], P('local', 'node'), may hold values from -6 to 6
- cotangent: bfloat16 [2048, 14336], P('local', 'node'), may hold values from -0.125 to 0.125
- gate_weight: bfloat16 [4096, 14336], P('local', 'node'), may hold values from -0.09375 to 0.09375
- up_weight: bfloat16 [4096, 14336], P('local', 'node'), may hold values from -0.09375 to 0.09375
- gate_first: bfloat16 [4096, 14336], P('local', 'node'), may hold values from -3 to 3
- up_first: bfloat16 [4096, 14336], P('local', 'node'), may hold values from -3 to 3
- gate_second: bfloat16 [4096, 14336], P('local', 'node'), may hold values from 0.00029945374 to 0.029907227
- up_second: bfloat16 [4096, 14336], P('local', 'node'), may hold values from 0.00029945374 to 0.029907227
Outputs:
- input_grad: bfloat16 [2048, 4096], P('local', 'node')
- gate_new: bfloat16 [4096, 14336], P('local', 'node')
- up_new: bfloat16 [4096, 14336], P('local', 'node')
- gate_first_new: bfloat16 [4096, 14336], P('local', 'node')
- up_first_new: bfloat16 [4096, 14336], P('local', 'node')
- gate_second_new: bfloat16 [4096, 14336], P('local', 'node')
- up_second_new: bfloat16 [4096, 14336], P('local', 'node')
All inputs are finite; a program needn't handle non-finite values.
Results may differ from a plain program's by a relative error of at most 0.0049.
Values may be sent and summed in bfloat16 or wider, within the bound.
A program may use at most 64 MiB of HBM per device.

v0:
```python
import jax
import jax.numpy as jnp
from jax import lax
from jax.sharding import PartitionSpec as P

first_decay = 0.9
second_decay = 0.999
learn_rate = 0.001
adam_eps = 1e-08
step_count = 10


def adam_update(weight, first, second, grad):
    first_new = first_decay * first.astype(jnp.float32) + (1.0 - first_decay) * grad
    second_new = second_decay * second.astype(jnp.float32) + (1.0 - second_decay) * grad * grad
    first_hat = first_new / (1.0 - first_decay**step_count)
    second_hat = second_new / (1.0 - second_decay**step_count)
    weight_new = weight.astype(jnp.float32) - learn_rate * first_hat / (
        jnp.sqrt(second_hat) + adam_eps
    )
    return (
        weight_new.astype(jnp.bfloat16),
        first_new.astype(jnp.bfloat16),
        second_new.astype(jnp.bfloat16),
    )


def contract_tokens(left, right):
    return lax.dot_general(
        left, right, (((0,), (0,)), ((), ())), preferred_element_type=jnp.float32
    )


def shards(tokens, cotangent, gate_weight, up_weight, gate_first, up_first, gate_second, up_second):
    features = lax.all_gather(tokens, "node", axis=1, tiled=True)
    gate_full, up_full = (
        lax.all_gather(gate_weight, "local", axis=0, tiled=True),
        lax.all_gather(up_weight, "local", axis=0, tiled=True),
    )
    gate_pre = jnp.dot(features, gate_full, preferred_element_type=jnp.float32)
    up_pre = jnp.dot(features, up_full, preferred_element_type=jnp.float32)
    sigmoid_gate = jax.nn.sigmoid(gate_pre)
    upstream = cotangent.astype(jnp.float32)
    gate_grad = (upstream * up_pre * sigmoid_gate * (1.0 + gate_pre * (1.0 - sigmoid_gate))).astype(
        jnp.bfloat16
    )
    up_grad = (upstream * gate_pre * sigmoid_gate).astype(jnp.bfloat16)
    partial_sum = lax.dot_general(
        gate_grad, gate_full, (((1,), (1,)), ((), ())), preferred_element_type=jnp.float32
    )
    partial_sum = partial_sum + lax.dot_general(
        up_grad, up_full, (((1,), (1,)), ((), ())), preferred_element_type=jnp.float32
    )
    input_grad = lax.psum_scatter(partial_sum, "node", scatter_dimension=1, tiled=True).astype(
        jnp.bfloat16
    )
    columns = lax.all_to_all(features, "local", split_axis=1, concat_axis=0, tiled=True)
    gate_all = lax.all_gather(gate_grad, "local", axis=0, tiled=True)
    up_all = lax.all_gather(up_grad, "local", axis=0, tiled=True)
    gate_wgrad = contract_tokens(columns, gate_all)
    up_wgrad = contract_tokens(columns, up_all)
    gate_new, gate_first_new, gate_second_new = adam_update(
        gate_weight, gate_first, gate_second, gate_wgrad
    )
    up_new, up_first_new, up_second_new = adam_update(up_weight, up_first, up_second, up_wgrad)
    return (
        input_grad,
        gate_new,
        up_new,
        gate_first_new,
        up_first_new,
        gate_second_new,
        up_second_new,
    )


def solution(mesh):
    in_specs = (
        P("local", "node"),
        P("local", "node"),
        P("local", "node"),
        P("local", "node"),
        P("local", "node"),
        P("local", "node"),
        P("local", "node"),
        P("local", "node"),
    )
    out_specs = (
        P("local", "node"),
        P("local", "node"),
        P("local", "node"),
        P("local", "node"),
        P("local", "node"),
        P("local", "node"),
        P("local", "node"),
    )
    return jax.shard_map(shards, mesh=mesh, in_specs=in_specs, out_specs=out_specs, check_vma=False)
```

profile of v0, /device:TPU:1, one launch (start us, length us, event | category | flops | bytes accessed | tf_op | source)
XLA Modules:
  0.0 535.0 jit_solution(1435949480019180687)
XLA Ops:
  7.2 0.0 copy-start.9
  7.2 0.0 all-gather.6.cloned.1.call-start
  7.2 1.5 copy.15
  8.7 0.0 all-gather.6.cloned.1.call-update
  8.7 0.0 all-gather.10.cloned.1.call-start
  8.8 0.7 all-gather.10.cloned.1.call-update
  9.5 0.0 all-gather.8.cloned.1.call-start
  9.5 0.7 all-gather.8.cloned.1.call-update
  10.2 0.0 all-gather.12.cloned.1.call-start
  10.3 73.2 %all-gather.6.cloned.1.call-done = bf16[128,4096]{0,1:T(8,128)(2,1)} async-done(((bf16[128,128]{0,1:T(8,128)(2,1)}), bf16[128,4096]{0,1:T(8,128)(2,1)}) %all-gather.6.cloned.1.call-update) | async-done | bytes 1048592 | tf_op jit(solution)/shard_map/all_gather | solution.py:35
  83.5 0.0 copy-start.1
  83.5 84.6 %all-gather.10.cloned.1.call-done = bf16[4096,448]{0,1:T(8,128)(2,1)} async-done(((bf16[256,448]{0,1:T(8,128)(2,1)}), bf16[4096,448]{0,1:T(8,128)(2,1)}) %all-gather.10.cloned.1.call-update) | async-done | bytes 3670032 | tf_op jit(solution)/shard_map/all_gather | solution.py:37
  168.0 4.1 fusion.10
  172.2 81.0 %all-gather.8.cloned.1.call-done = bf16[4096,448]{0,1:T(8,128)(2,1)} async-done(((bf16[256,448]{0,1:T(8,128)(2,1)}), bf16[4096,448]{0,1:T(8,128)(2,1)}) %all-gather.8.cloned.1.call-update) | async-done | bytes 3670032 | tf_op jit(solution)/shard_map/all_gather | solution.py:38
  253.2 0.0 copy-done.9
  253.2 0.0 copy-done.1
  253.2 3.8 fusion.2
  257.0 0.0 copy-start.2
  257.0 0.0 all-gather.12.cloned.1.call-update
  257.1 0.0 all-gather.14.cloned.1.call-start
  257.1 0.5 all-gather.14.cloned.1.call-update
  257.6 0.0 reduce-scatter.2.cloned.1.call-start
  257.7 0.0 copy-start
  257.7 3.0 fusion.11
  260.7 0.0 copy-done.2
  260.7 0.2 copy-done
  260.9 2.1 convolution_add_fusion
  263.0 0.0 copy-start.3
  263.0 0.0 copy-start.5
  263.0 0.0 copy-start.6
  263.0 0.0 reduce-scatter.2.cloned.1.call-update
  263.0 32.3 %all_to_all.19 = bf16[128,16,256]{0,2,1:T(8,128)(2,1)S(1)} all-to-all(bf16[128,16,256]{0,2,1:T(8,128)(2,1)S(1)} %bitcast.20), channel_id=1, replica_groups=mesh['node'=32,'local'=16] {'local'}, dimensions={1} | all-to-all | bytes 2097152 | tf_op jit(solution)/shard_map/all_to_all | solution.py:57
  295.3 0.5 copy.16
  295.8 41.7 %all-gather.12.cloned.1.call-done = bf16[2048,448]{0,1:T(8,128)(2,1)} async-done(((bf16[128,448]{0,1:T(8,128)(2,1)}), bf16[2048,448]{0,1:T(8,128)(2,1)}) %all-gather.12.cloned.1.call-update) | async-done | bytes 1835024 | tf_op jit(solution)/shard_map/all_gather | solution.py:58
  337.6 0.0 copy-done.3
  337.6 0.0 copy-done.5
  337.6 0.0 copy-done.6
  337.6 0.0 copy-start.4
  337.6 0.0 copy-start.7
  337.6 0.0 copy-start.8
  337.6 3.3 fusion.8
  340.9 65.0 %all-gather.14.cloned.1.call-done = bf16[2048,448]{0,1:T(8,128)(2,1)} async-done(((bf16[128,448]{0,1:T(8,128)(2,1)}), bf16[2048,448]{0,1:T(8,128)(2,1)}) %all-gather.14.cloned.1.call-update) | async-done | bytes 1835024 | tf_op jit(solution)/shard_map/all_gather | solution.py:59
  405.9 0.0 copy-done.4
  405.9 0.0 copy-done.7
  405.9 0.0 copy-done.8
  405.9 3.3 fusion.7
  409.2 117.5 %reduce-scatter.2.cloned.1.call-done = f32[128,128]{1,0:T(8,128)} async-done(((f32[128,4096]{1,0:T(8,128)}), f32[128,128]{1,0:T(8,128)}) %reduce-scatter.2.cloned.1.call-update) | async-done | bytes 65552 | tf_op jit(solution)/shard_map/reduce_scatter | solution.py:54
  526.7 1.5 convert_element_type.51
Async XLA Ops:
  7.2 246.1 %copy-start.9 = (bf16[128,448]{0,1:T(8,128)(2,1)S(1)}, bf16[128,448]{0,1:T(8,128)(2,1)}, u32[]{:S(2)}) copy-start(bf16[128,448]{0,1:T(8,128)(2,1)} %param.9) | copy-start | bytes 344068
  7.2 76.3 %all-gather.6.cloned.1.call-start = ((), (), s32[]{:S(2)}) async-start(), calls=%async_computation.2 | async-start | bytes 1081344 | tf_op jit(solution)/shard_map/all_gather | solution.py:35
  8.7 159.3 %all-gather.10.cloned.1.call-start = ((), (), s32[]{:S(2)}) async-start(), calls=%async_computation.4 | async-start | bytes 3899392 | tf_op jit(solution)/shard_map/all_gather | solution.py:37
  9.5 243.7 %all-gather.8.cloned.1.call-start = ((), (), s32[]{:S(2)}) async-start(), calls=%async_computation.3 | async-start | bytes 3899392 | tf_op jit(solution)/shard_map/all_gather | solution.py:38
  10.2 327.4 %all-gather.12.cloned.1.call-start = ((), (), s32[]{:S(2)}) async-start(), calls=%async_computation.6 | async-start | bytes 1949696 | tf_op jit(solution)/shard_map/all_gather | solution.py:58
  83.5 169.8 %copy-start.1 = (bf16[128,4096]{0,1:T(8,128)(2,1)S(1)}, bf16[128,4096]{0,1:T(8,128)(2,1)}, u32[]{:S(2)}) copy-start(bf16[128,4096]{0,1:T(8,128)(2,1)} %all-gather.6.cloned.1.call-done) | copy-start | bytes 3145732
  257.0 3.7 copy-start.2
  257.1 148.9 %all-gather.14.cloned.1.call-start = ((), (), s32[]{:S(2)}) async-start(), calls=%async_computation.7 | async-start | bytes 1949696 | tf_op jit(solution)/shard_map/all_gather | solution.py:59
  257.6 269.1 %reduce-scatter.2.cloned.1.call-start = ((), (), s32[]{:S(2)}) async-start(), calls=%async_computation.5 | async-start | bytes 2162688 | tf_op jit(solution)/shard_map/reduce_scatter | solution.py:54
  257.7 3.2 copy-start
  263.0 74.6 %copy-start.3 = (bf16[256,448]{0,1:T(8,128)(2,1)S(1)}, bf16[256,448]{0,1:T(8,128)(2,1)}, u32[]{:S(2)}) copy-start(bf16[256,448]{0,1:T(8,128)(2,1)} %param.10) | copy-start | bytes 688132
  263.0 74.6 %copy-start.5 = (bf16[256,448]{0,1:T(8,128)(2,1)S(1)}, bf16[256,448]{0,1:T(8,128)(2,1)}, u32[]{:S(2)}) copy-start(bf16[256,448]{0,1:T(8,128)(2,1)} %param.14) | copy-start | bytes 688132
  263.0 74.6 %copy-start.6 = (bf16[256,448]{0,1:T(8,128)(2,1)S(1)}, bf16[256,448]{0,1:T(8,128)(2,1)}, u32[]{:S(2)}) copy-start(bf16[256,448]{0,1:T(8,128)(2,1)} %param.12) | copy-start | bytes 688132
  337.6 68.4 %copy-start.4 = (bf16[256,448]{0,1:T(8,128)(2,1)S(1)}, bf16[256,448]{0,1:T(8,128)(2,1)}, u32[]{:S(2)}) copy-start(bf16[256,448]{0,1:T(8,128)(2,1)} %param.11) | copy-start | bytes 688132
  337.6 68.4 %copy-start.7 = (bf16[256,448]{0,1:T(8,128)(2,1)S(1)}, bf16[256,448]{0,1:T(8,128)(2,1)}, u32[]{:S(2)}) copy-start(bf16[256,448]{0,1:T(8,128)(2,1)} %param.15) | copy-start | bytes 688132
  337.6 68.3 %copy-start.8 = (bf16[256,448]{0,1:T(8,128)(2,1)S(1)}, bf16[256,448]{0,1:T(8,128)(2,1)}, u32[]{:S(2)}) copy-start(bf16[256,448]{0,1:T(8,128)(2,1)} %param.13) | copy-start | bytes 688132
Sparse Core Ops, SparseCore 0:
  10.7 72.6 all-gather.5
  86.4 81.5 all-gather.9
  171.0 82.1 all-gather.7
  257.2 80.3 all-gather.11
  341.0 64.9 all-gather.13
  408.6 118.0 reduce-scatter.1
where the time goes:
time: 538 us; the launch traced here: 535 us
  waiting for transfers between devices  465 us (86%)
  blocking collectives  32.3 us (6%)
  matrix products  19.6 us (4%)
  between operations  14.2 us (3%)
    reduce_scatter x1, waiting for transfers between devices, shards(): lax.psum_scatter(partial_sum, 'node', scatter_dimension=1, tiled=True)  118 us
    all_gather x1, waiting for transfers between devices, shards(): lax.all_gather(gate_weight, 'local', axis=0, tiled=True)  84.6 us
    all_gather x1, waiting for transfers between devices, shards(): lax.all_gather(up_weight, 'local', axis=0, tiled=True)  81 us
    all_gather x1, waiting for transfers between devices, shards(): features = lax.all_gather(tokens, 'node', axis=1, tiled=True)  73.2 us
    all_gather x1, waiting for transfers between devices, shards(): up_all = lax.all_gather(up_grad, 'local', axis=0, tiled=True)  65 us
    all_gather x1, waiting for transfers between devices, shards(): gate_all = lax.all_gather(gate_grad, 'local', axis=0, tiled=True)  41.7 us
    all_to_all x1, blocking collectives, shards(): lax.all_to_all(features, 'local', split_axis=1, concat_axis=0, tiled=True)  32.3 us
  transfers between devices with their start and end apart: 6, of which 6 were waited for; matrix products, arithmetic and copies ran while one was open for 3% of the time, Pallas kernels for 0%

commit v1 on v0

v1 whole, which is shorter than its diff:
```python
import functools

import jax
import jax.numpy as jnp
from jax import lax
from jax.experimental import pallas as pl
from jax.experimental.pallas import tpu as pltpu
from jax.sharding import PartitionSpec as P

first_decay = 0.9
second_decay = 0.999
learn_rate = 0.001
adam_eps = 1e-08
step_count = 10

MESH = pl.DeviceIdType.MESH
bf16, f32 = jnp.bfloat16, jnp.float32

NT = 2
TB = 128 // NT
H = TB // 2
CHUNKS = ((0, 1), (2, 3))
NF = len(CHUNKS)
SEMS = 256


def tile_width(k):
    return 256 if k < 3 else 128


WIDTH = tuple(sum(tile_width(k) for k in tiles) for tiles in CHUNKS)


def adam_update(weight, first, second, grad):
    first_new = first_decay * first.astype(jnp.float32) + (1.0 - first_decay) * grad
    second_new = second_decay * second.astype(jnp.float32) + (1.0 - second_decay) * grad * grad
    first_hat = first_new / (1.0 - first_decay**step_count)
    second_hat = second_new / (1.0 - second_decay**step_count)
    weight_new = weight.astype(jnp.float32) - learn_rate * first_hat / (
        jnp.sqrt(second_hat) + adam_eps
    )
    return (
        weight_new.astype(jnp.bfloat16),
        first_new.astype(jnp.bfloat16),
        second_new.astype(jnp.bfloat16),
    )


def tiles_of(f):
    at = 0
    for k in CHUNKS[f]:
        yield k, at
        at += tile_width(k)


def kernel(tok, cot, gw, uw, dx_out, gg_out, ug_out, *scratch):
    names = list(SCRATCH)
    s = dict(zip(names, scratch))
    send, recv = s["send"], s["recv"]
    node, local = lax.axis_index("node"), lax.axis_index("local")
    z, w, c = node // 4, (node // 2) % 2, node % 2
    a, b = local // 4, local % 4

    def dev(x=a, y=b, zz=z, ww=w, cc=c):
        return (zz * 4 + ww * 2 + cc, x * 4 + y)

    right = {"x": dev(x=(a + 1) % 4), "y": dev(y=(b + 1) % 4)}
    left = {"x": dev(x=(a + 3) % 4), "y": dev(y=(b + 3) % 4)}
    partner = dev(cc=1 - c)
    is_sink = (z % 2) == (b // 2)

    count = [0]
    unsent = []

    def take(n=1):
        at = count[0]
        count[0] += n
        assert count[0] <= SEMS
        return at

    def put(src, dst, to, sem=None, sem_at=None):
        i = take() if sem is None else sem
        j = i if sem_at is None else sem_at
        copy = pltpu.make_async_remote_copy(
            src_ref=src, dst_ref=dst, send_sem=send.at[i], recv_sem=recv.at[j],
            device_id=to, device_id_type=MESH,
        )
        copy.start()
        unsent.append(copy)
        return copy

    def gather_start(buf, axis, half):
        lo, hi = pl.ds(0, half), pl.ds(half, half)
        r1 = put(buf.at[0, lo], buf.at[3, lo], right[axis])
        l1 = put(buf.at[0, hi], buf.at[1, hi], left[axis])
        r2 = put(buf.at[0, hi], buf.at[3, hi], right[axis])
        l2 = put(buf.at[0, lo], buf.at[1, lo], left[axis])
        return [buf, axis, half, r1, l1, r2, l2]

    def gather_relay(g):
        buf, axis, half, r1, l1, r2, l2 = g
        lo, hi = pl.ds(0, half), pl.ds(half, half)
        r1.wait_recv()
        r3 = put(buf.at[3, lo], buf.at[2, lo], right[axis])
        l1.wait_recv()
        l3 = put(buf.at[1, hi], buf.at[2, hi], left[axis])
        g += [r3, l3]

    def gather_finish(g):
        for copy in g[5:]:
            copy.wait_recv()

    def reduce_start(part, keep, mid_left, mid_right, from_left, from_right, axis, half):
        lo, hi = pl.ds(0, half), pl.ds(half, half)
        r1 = put(part.at[1, lo], mid_left, right[axis])
        l1 = put(part.at[1, hi], mid_right, left[axis])
        r2 = put(part.at[0, hi], from_left.at[hi], right[axis])
        l2 = put(part.at[2, lo], from_right.at[lo], left[axis])
        return [part, keep, mid_left, mid_right, from_left, from_right, axis, half, r1, l1, r2, l2]

    def reduce_relay(g):
        part, keep, mid_left, mid_right, from_left, from_right, axis, half, r1, l1, r2, l2 = g
        lo, hi = pl.ds(0, half), pl.ds(half, half)
        r1.wait_recv()
        part[0, :half] = (keep[0] + mid_left[...].astype(f32)).astype(bf16)
        r3 = put(part.at[0, lo], from_left.at[lo], right[axis])
        l1.wait_recv()
        part[2, half:] = (keep[1] + mid_right[...].astype(f32)).astype(bf16)
        l3 = put(part.at[2, hi], from_right.at[hi], left[axis])
        g += [r3, l3]

    def reduce_finish(g):
        for copy in g[10:]:
            copy.wait_recv()

    peers = [right["x"], left["x"], partner]
    peers += [dev(zz=(z + k) % 8) for k in range(1, 8)]
    peers += [dev(y=(b + k) % 4, ww=w) for k in range(1, 4)]
    peers += [dev(y=(b + k) % 4, ww=1 - w) for k in range(4)]
    barrier = pltpu.get_barrier_semaphore()
    for peer in peers:
        pl.semaphore_signal(barrier, inc=1, device_id=peer, device_id_type=MESH)
    pl.semaphore_wait(barrier, len(peers))

    held, X = s["held"], s["X"]
    home = 2 * (z % 2) + w
    slot = (b - home + 4) % 4
    held_sem = take(4)
    tok_sem = take(2)
    for wd in range(2):
        own = (home == b) & (w == wd)

        def tok_remote(to=dev(y=home, ww=wd), i=tok_sem + wd):
            return pltpu.make_async_remote_copy(
                src_ref=tok, dst_ref=held.at[slot], send_sem=send.at[i],
                recv_sem=recv.at[held_sem + slot], device_id=to, device_id_type=MESH,
            )

        @pl.when(own)
        def _():
            pltpu.make_async_copy(tok, held.at[0], recv.at[held_sem]).start()

        @pl.when(jnp.logical_not(own))
        def _():
            tok_remote().start()

    W = [s[f"W{f}"] for f in range(NF)]
    w_gather = []
    for f in range(NF):
        for k, at in tiles_of(f):
            if k < 3:
                W[f][0, :, at:at + 128] = gw[:, 128 * k:128 * k + 128]
                W[f][0, :, at + 128:at + 256] = uw[:, 128 * k:128 * k + 128]
            else:
                W[f][0, :, at:at + 128] = jnp.concatenate([gw[:, 384:448], uw[:, 384:448]], axis=1)
        w_gather.append(gather_start(W[f], "x", 128))

    column = (z // 2 - a + 4) % 4
    z_sem = take(4 * NT)
    z_send = take(7 * NT)

    def z_dst(h, j):
        return X.at[h, :, :, pl.ds(pl.multiple_of((2 * j + c) * 128, 128), 128)]

    def z_copy(h, k):
        return pltpu.make_async_remote_copy(
            src_ref=held.at[:, pl.ds(h * TB, TB)], dst_ref=z_dst(h, column),
            send_sem=send.at[z_send + h * 7 + k - 1], recv_sem=recv.at[z_sem + 4 * h + column],
            device_id=dev(zz=(z + k) % 8), device_id_type=MESH,
        )

    @pl.when(is_sink)
    def _():
        for r in range(4):
            pltpu.make_async_copy(tok, held.at[r], recv.at[held_sem + r]).wait()
        for h in range(NT):
            pltpu.make_async_copy(
                held.at[:, pl.ds(h * TB, TB)], z_dst(h, column), recv.at[z_sem + 4 * h + column]
            ).start()
            for k in (1, 7, 2, 6, 3, 5, 4):
                z_copy(h, k).start()

    def x_relay(h):
        copies = []
        for j in range(4):
            pltpu.make_async_copy(
                held.at[:, pl.ds(h * TB, TB)], z_dst(h, j), recv.at[z_sem + 4 * h + j]
            ).wait()
            copies.append(put(z_dst(h, j), z_dst(h, j), partner))
        return copies

    units = [(h, f) for h in range(NT) for f in range(NF)]
    pre_reduce, g_gather, w_reduce = {}, {}, {}

    def project(h, f):
        x = X[h].reshape(4 * TB, 1024)
        out = jnp.dot(x, W[f][...].reshape(1024, WIDTH[f]), preferred_element_type=f32)
        out = out.reshape(4, TB, WIDTH[f])
        s[f"own{f}"][h] = out[0]
        part, keep = s[f"part{f}"].at[h], s[f"keep{f}"].at[h]
        part[1] = out[2].astype(bf16)
        part[0, H:] = out[1, H:].astype(bf16)
        part[2, :H] = out[3, :H].astype(bf16)
        keep[0] = out[1, :H]
        keep[1] = out[3, H:]
        pre_reduce[h, f] = reduce_start(
            part, keep, s[f"midl{f}"].at[h], s[f"midr{f}"].at[h],
            s[f"finl{f}"].at[h], s[f"finr{f}"].at[h], "y", H,
        )

    def pointwise(gp, up, ct):
        sg = jax.nn.sigmoid(gp)
        cs = ct * sg
        return cs * up * (1.0 + gp * (1.0 - sg)), cs * gp

    def gate(h, f):
        reduce_finish(pre_reduce[h, f])
        pre = s[f"own{f}"][h] + s[f"finl{f}"][h].astype(f32) + s[f"finr{f}"][h].astype(f32)
        rows = slice(h * TB, h * TB + TB)
        G = s[f"G{f}"]
        for k, at in tiles_of(f):
            if k < 3:
                ct = cot[rows, 128 * k:128 * k + 128].astype(f32)
                gg, ug = pointwise(pre[:, at:at + 128], pre[:, at + 128:at + 256], ct)
                G[h, 0, :, at:at + 128] = gg.astype(bf16)
                G[h, 0, :, at + 128:at + 256] = ug.astype(bf16)
            else:
                ct = cot[rows, 384:448].astype(f32)
                ct = jnp.concatenate([ct, ct], axis=1)
                both = pre[:, at:at + 128]
                gg, ug = pointwise(both, pltpu.roll(both, 64, 1), ct)
                lane = lax.broadcasted_iota(jnp.int32, gg.shape, 1)
                G[h, 0, :, at:at + 128] = jnp.where(lane < 64, gg, pltpu.roll(ug, 64, 1)).astype(bf16)
        g_gather[h, f] = gather_start(G.at[h], "y", H)

    acc = s["acc"]

    def input_grad(h, f):
        gather_finish(g_gather[h, f])
        g = s[f"G{f}"][h].reshape(4 * TB, WIDTH[f])
        out = lax.dot_general(
            g, W[f][...].reshape(1024, WIDTH[f]), (((1,), (1,)), ((), ())),
            preferred_element_type=f32,
        )
        for k in range(8):
            if f == 0:
                acc[h, k] = out[:, 128 * k:128 * k + 128]
            else:
                acc[h, k] += out[:, 128 * k:128 * k + 128]

    core_recv, sink_send, sink_recv = (s[n] for n in ("cr", "zs", "zr"))
    core_copies = {}

    def dx_core(h):
        core_copies[h] = []
        for j in range(4):
            core_copies[h].append(put(acc.at[h, 2 * j + 1 - c], core_recv.at[h, j], partner))

    dx_sem = take(8 * NT)
    dx_send = take(4 * NT)

    def sink_copy(h, j):
        zj = 2 * ((a + j) % 4) + b // 2
        k = (z - zj + 8) % 8
        remote = pltpu.make_async_remote_copy(
            src_ref=sink_send.at[h, j], dst_ref=sink_recv.at[h, k],
            send_sem=send.at[dx_send + 4 * h + j], recv_sem=recv.at[dx_sem + 8 * h + k],
            device_id=dev(zz=zj), device_id_type=MESH,
        )
        return zj, remote

    def dx_sinks(h):
        for j in range(4):
            core_copies[h][j].wait_recv()
            sink_send[h, j] = (acc[h, 2 * j + c] + core_recv[h, j]).astype(bf16)
            zj, remote = sink_copy(h, j)

            @pl.when(zj == z)
            def _():
                pltpu.make_async_copy(
                    sink_send.at[h, j], sink_recv.at[h, 0], recv.at[dx_sem + 8 * h]
                ).start()

            @pl.when(zj != z)
            def _():
                remote.start()

    last_send, last_recv = s["ls"], s["lr"]
    out_sem = take(2 * NT)
    out_send = take(4 * NT)

    def out_copy(h, r):
        return pltpu.make_async_remote_copy(
            src_ref=last_send.at[h, pl.ds(r * TB, TB)], dst_ref=last_recv.at[h, w],
            send_sem=send.at[out_send + 4 * h + r], recv_sem=recv.at[out_sem + 2 * h + w],
            device_id=dev(y=(b + r) % 4, ww=b % 2), device_id_type=MESH,
        )

    def dx_spread(h):
        @pl.when(is_sink)
        def _():
            total = None
            for k in range(8):
                pltpu.make_async_copy(
                    sink_send.at[h, 0], sink_recv.at[h, k], recv.at[dx_sem + 8 * h + k]
                ).wait()
                term = sink_recv[h, k].astype(f32)
                total = term if total is None else total + term
            last_send[h] = total
            for r in range(4):
                if r:
                    out_copy(h, r).start()
                else:
                    @pl.when(w == b % 2)
                    def _():
                        pltpu.make_async_copy(
                            last_send.at[h, pl.ds(0, TB)], last_recv.at[h, w],
                            recv.at[out_sem + 2 * h + w],
                        ).start()

                    @pl.when(w != b % 2)
                    def _():
                        out_copy(h, 0).start()

    def dx_finish(h):
        for ww in range(2):
            pltpu.make_async_copy(
                last_send.at[h, pl.ds(0, TB)], last_recv.at[h, ww], recv.at[out_sem + 2 * h + ww]
            ).wait()
        dx_out[h * TB:h * TB + TB] = (last_recv[h, 0] + last_recv[h, 1]).astype(bf16)

    def weight_grad(f):
        g = s[f"G{f}"][...].reshape(512, WIDTH[f])
        for j in (2, 1, 3, 0):
            x = X[:, :, :, 256 * j:256 * j + 256].reshape(512, 256)
            out = lax.dot_general(x, g, (((0,), (0,)), ((), ())), preferred_element_type=f32)
            if j == 2:
                s[f"wp{f}"][1] = out.astype(bf16)
            elif j == 1:
                s[f"wp{f}"][0, 128:] = out[128:].astype(bf16)
                s[f"wk{f}"][0] = out[:128]
            elif j == 3:
                s[f"wp{f}"][2, :128] = out[:128].astype(bf16)
                s[f"wk{f}"][1] = out[128:]
            else:
                s[f"wo{f}"][...] = out
            if j == 3:
                w_reduce[f] = reduce_start(
                    s[f"wp{f}"], s[f"wk{f}"], s[f"wml{f}"], s[f"wmr{f}"], s[f"wfl{f}"], s[f"wfr{f}"], "x", 128
                )

    def weight_finish(f):
        reduce_finish(w_reduce[f])
        total = s[f"wo{f}"][...] + s[f"wfl{f}"][...].astype(f32) + s[f"wfr{f}"][...].astype(f32)
        for k, at in tiles_of(f):
            if k < 3:
                gg_out[:, 128 * k:128 * k + 128] = total[:, at:at + 128]
                ug_out[:, 128 * k:128 * k + 128] = total[:, at + 128:at + 256]
            else:
                both = total[:, at:at + 128]
                gg_out[:, 384:448] = both[:, :64]
                ug_out[:, 384:448] = pltpu.roll(both, 64, 1)[:, :64]

    def ready(copies):
        for copy in copies:
            copy.wait_recv()

    gather_relay(w_gather[0])
    x0 = x_relay(0)
    gather_relay(w_gather[1])
    gather_finish(w_gather[0])
    ready(x0)
    project(0, 0)
    gather_finish(w_gather[1])
    project(0, 1)
    reduce_relay(pre_reduce[0, 0])
    reduce_relay(pre_reduce[0, 1])
    x1 = x_relay(1)
    ready(x1)
    project(1, 0)
    project(1, 1)
    gate(0, 0)
    gate(0, 1)
    gather_relay(g_gather[0, 0])
    gather_relay(g_gather[0, 1])
    reduce_relay(pre_reduce[1, 0])
    reduce_relay(pre_reduce[1, 1])
    input_grad(0, 0)
    input_grad(0, 1)
    dx_core(0)
    gate(1, 0)
    dx_sinks(0)
    gate(1, 1)
    gather_relay(g_gather[1, 0])
    gather_relay(g_gather[1, 1])
    dx_spread(0)
    input_grad(1, 0)
    weight_grad(0)
    input_grad(1, 1)
    dx_core(1)
    weight_grad(1)
    dx_sinks(1)
    reduce_relay(w_reduce[0])
    dx_finish(0)
    reduce_relay(w_reduce[1])
    dx_spread(1)
    weight_finish(0)
    dx_finish(1)
    weight_finish(1)

    for copy in unsent:
        copy.wait_send()
    for wd in range(2):
        @pl.when(jnp.logical_not((home == b) & (w == wd)))
        def _():
            pltpu.make_async_remote_copy(
                src_ref=tok, dst_ref=held.at[slot], send_sem=send.at[tok_sem + wd],
                recv_sem=recv.at[held_sem + slot], device_id=dev(y=home, ww=wd),
                device_id_type=MESH,
            ).wait_send()

    for h in range(NT):
        for j in range(4):
            zj, remote = sink_copy(h, j)

            @pl.when(zj != z)
            def _():
                remote.wait_send()

    @pl.when(is_sink)
    def _():
        for h in range(NT):
            for k in range(1, 8):
                z_copy(h, k).wait_send()
            for r in range(1, 4):
                out_copy(h, r).wait_send()

            @pl.when(w != b % 2)
            def _():
                out_copy(h, 0).wait_send()


def scratch_shapes():
    V = pltpu.VMEM
    shapes = {
        "held": V((4, 128, 128), bf16),
        "X": V((NT, 4, TB, 1024), bf16),
        "acc": V((NT, 8, 4 * TB, 128), f32),
        "cr": V((NT, 4, 4 * TB, 128), f32),
        "zs": V((NT, 4, 4 * TB, 128), bf16),
        "zr": V((NT, 8, 4 * TB, 128), bf16),
        "ls": V((NT, 4 * TB, 128), f32),
        "lr": V((NT, 2, TB, 128), f32),
    }
    for f in range(NF):
        n = WIDTH[f]
        shapes[f"W{f}"] = V((4, 256, n), bf16)
        shapes[f"G{f}"] = V((NT, 4, TB, n), bf16)
        shapes[f"own{f}"] = V((NT, TB, n), f32)
        shapes[f"part{f}"] = V((NT, 3, TB, n), bf16)
        shapes[f"keep{f}"] = V((NT, 2, H, n), f32)
        shapes[f"midl{f}"] = V((NT, H, n), bf16)
        shapes[f"midr{f}"] = V((NT, H, n), bf16)
        shapes[f"finl{f}"] = V((NT, TB, n), bf16)
        shapes[f"finr{f}"] = V((NT, TB, n), bf16)
        shapes[f"wo{f}"] = V((256, n), f32)
        shapes[f"wp{f}"] = V((3, 256, n), bf16)
        shapes[f"wk{f}"] = V((2, 128, n), f32)
        shapes[f"wml{f}"] = V((128, n), bf16)
        shapes[f"wmr{f}"] = V((128, n), bf16)
        shapes[f"wfl{f}"] = V((256, n), bf16)
        shapes[f"wfr{f}"] = V((256, n), bf16)
    shapes["send"] = pltpu.SemaphoreType.DMA((SEMS,))
    shapes["recv"] = pltpu.SemaphoreType.DMA((SEMS,))
    return shapes


SCRATCH = scratch_shapes()


def gradients(tokens, cotangent, gate_weight, up_weight):
    vmem = pl.BlockSpec(memory_space=pltpu.VMEM)
    return pl.pallas_call(
        kernel,
        out_shape=(
            jax.ShapeDtypeStruct((128, 128), bf16),
            jax.ShapeDtypeStruct((256, 448), f32),
            jax.ShapeDtypeStruct((256, 448), f32),
        ),
        in_specs=[vmem] * 4,
        out_specs=(vmem,) * 3,
        scratch_shapes=list(SCRATCH.values()),
        compiler_params=pltpu.CompilerParams(
            collective_id=0, has_side_effects=True, vmem_limit_bytes=48 << 20
        ),
        cost_estimate=pl.CostEstimate(
            flops=2_818_572_288, bytes_accessed=2_000_000, transcendentals=57344
        ),
    )(tokens, cotangent, gate_weight, up_weight)


def shards(tokens, cotangent, gate_weight, up_weight, gate_first, up_first, gate_second, up_second):
    input_grad, gate_wgrad, up_wgrad = gradients(tokens, cotangent, gate_weight, up_weight)
    gate_new, gate_first_new, gate_second_new = adam_update(
        gate_weight, gate_first, gate_second, gate_wgrad
    )
    up_new, up_first_new, up_second_new = adam_update(up_weight, up_first, up_second, up_wgrad)
    return (
        input_grad,
        gate_new,
        up_new,
        gate_first_new,
        up_first_new,
        gate_second_new,
        up_second_new,
    )


def solution(mesh):
    spec = P("local", "node")
    return jax.shard_map(
        shards, mesh=mesh, in_specs=(spec,) * 8, out_specs=(spec,) * 7, check_vma=False
    )
```

time: 538 us -> 111 us (0.21)
  waiting for transfers between devices: 465 us -> 0 us
  Pallas kernels: 0 us -> 94.8 us
  blocking collectives: 32.3 us -> 0 us
  matrix products: 19.6 us -> 0 us
  between operations: 14.2 us -> 0.72 us
  local copies, waits for them, and re-layouts: 2.24 us -> 12.9 us
    all_gather x5 -> x0, waiting for transfers between devices: 346 us -> none  [the longest x1 84.6 us: shards(): lax.all_gather(gate_weight, 'local', axis=0, tiled=True)]
    reduce_scatter x1 -> x0, waiting for transfers between devices: 118 us -> none  [shards(): lax.psum_scatter(partial_sum, 'node', scatter_dimension=1, tiled=True)]
    pallas_call x0 -> x1, Pallas kernels: none -> 94.8 us  [gradients(): pl.pallas_call(kernel, out_shape=(jax.ShapeDtypeStruct((128, 128), bf16),...]
    all_to_all x1 -> x0, blocking collectives: 32.3 us -> none  [shards(): lax.all_to_all(features, 'local', split_axis=1, concat_axis=0, tiled=True)]
    dot_general x6 -> x0, matrix products: 19.6 us -> none  [the longest x2 6.59 us: contract_tokens(): lax.dot_general(left, right, (((0,), (0,)), ((), ())), preferred_element_...]
    unnamed x21 -> x28, local copies, waits for them, and re-layouts: 1.72 us -> 12.9 us
  transfers between devices with their start and end apart: 6 -> 0, of which waited for: 6 -> 0; matrix products, arithmetic and copies ran while one was open for 3% -> 0% of each run, Pallas kernels for 0% -> 0%
where the time goes in v1:
time: 111 us
  Pallas kernels  94.8 us (85%)
  local copies, waits for them, and re-layouts  12.9 us (12%)
  other arithmetic  2.65 us (2%)
    pallas_call x1, Pallas kernels, gradients(): pl.pallas_call(kernel, out_shape=(jax.ShapeDtypeStruct((128, 128), bf16),...  94.8 us
    unnamed x28, local copies, waits for them, and re-layouts  12.9 us
    convert_element_type x1, other arithmetic, adam_update(): second_new.astype(jnp.bfloat16)  2.65 us

profile of v1, /device:TPU:1, one launch (start us, length us, event | category | flops | bytes accessed | tf_op | source)
XLA Modules:
  0.0 111.1 jit_solution(5296822271714114187)
XLA Ops:
  0.6 0.0 copy-start.1
  0.6 1.0 copy.15.cot
  1.7 0.0 copy-done.1
  1.7 0.0 copy-start.2
  1.7 0.1 copy.16.gw
  1.9 0.8 copy-done.2
  2.6 0.0 copy-start
  2.6 0.1 copy.17.uw
  2.8 0.6 copy-done
  3.4 0.0 copy-start.3
  3.4 94.8 %shard_map.135 = (bf16[128,128]{1,0:T(8,128)(2,1)S(1)}, f32[256,448]{1,0:T(8,128)S(1)}, f32[256,448]{1,0:T(8,128)S(1)}) custom-call(bf16[128,128]{1,0:T(8,128)(2,1)S(1)} %copy-done, bf16[128,448]{1,0:T(8,128)(2,1)S(1)} %copy.15.cot, bf16[256,448]{1,0:T(8,128)(2,1)S(1)} %copy.16.gw, bf16[256,448]{1,0:T(8,128)(2,1)S(1)} %copy.17.uw), custom_call_target="tpu_custom_call" | custom-call | flops 2818572288 | bytes 2000000 | tf_op jit(solution)/shard_map/pallas_call | solution.py:503
  98.2 0.0 copy-done.3
  98.2 0.0 copy-start.4
  98.3 0.1 copy.23
  98.4 0.8 copy-done.4
  99.2 0.0 copy-start.5
  99.2 0.1 copy.22
  99.3 0.8 copy-done.5
  100.1 0.0 copy-start.6
  100.1 0.9 copy.19
  101.0 0.1 copy-done.6
  101.1 0.8 copy.20
  101.9 2.6 %fusion.4 = (bf16[256,448]{1,0:T(8,128)(2,1)S(1)}, bf16[256,448]{1,0:T(8,128)(2,1)S(1)}, bf16[256,448]{1,0:T(8,128)(2,1)S(1)}, bf16[256,448]{1,0:T(8,128)(2,1)S(...) fusion(f32[256,448]{1,0:T(8,128)S(1)} %get-tuple-element.12, bf16[256,448]{1,0:T(8,128)(2,1)S(1)} %copy.23, ...), kind=kLoop, calls=%fused_computation.10 | loop fusion | flops 4128768 | bytes 3670016 | tf_op jit(solution)/shard_map/convert_element_type | solution.py:45
  104.5 1.8 %copy.24 = bf16[256,448]{0,1:T(8,128)(2,1)} copy(bf16[256,448]{1,0:T(8,128)(2,1)} %get-tuple-element.27) | data formatting | bytes 458752
  106.3 0.8 copy.25
  107.1 0.8 copy.26
  108.0 0.8 copy.27
  108.8 0.8 copy.28
  109.6 0.8 copy.29
  110.5 0.6 copy.31
Async XLA Ops:
  0.6 1.1 copy-start.1
  1.7 0.9 copy-start.2
  2.6 0.8 copy-start
  3.4 94.8 %copy-start.3 = (bf16[256,448]{0,1:T(8,128)(2,1)S(1)}, bf16[256,448]{0,1:T(8,128)(2,1)}, u32[]{:S(2)}) copy-start(bf16[256,448]{0,1:T(8,128)(2,1)} %param.15) | copy-start | bytes 688132
  98.2 0.9 copy-start.4
  99.2 0.9 copy-start.5
  100.1 0.9 copy-start.6

commit v2 on v1

--- a/solution.py
+++ b/solution.py
@@ -53,7 +53,7 @@
         at += tile_width(k)
 
 
-def kernel(tok, cot, gw, uw, dx_out, gg_out, ug_out, *scratch):
+def kernel(tok, cot_t, gw, uw, dx_out, gg_out, ug_out, *scratch):
     names = list(SCRATCH)
     s = dict(zip(names, scratch))
     send, recv = s["send"], s["recv"]
@@ -70,7 +70,7 @@
     is_sink = (z % 2) == (b // 2)
 
     count = [0]
-    unsent = []
+    leaving = []
 
     def take(n=1):
         at = count[0]
@@ -86,7 +86,7 @@
             device_id=to, device_id_type=MESH,
         )
         copy.start()
-        unsent.append(copy)
+        leaving.append(copy.wait_send)
         return copy
 
     def gather_start(buf, axis, half):
@@ -149,6 +149,7 @@
     tok_sem = take(2)
     for wd in range(2):
         own = (home == b) & (w == wd)
+        away = jnp.logical_not(own)
 
         def tok_remote(to=dev(y=home, ww=wd), i=tok_sem + wd):
             return pltpu.make_async_remote_copy(
@@ -160,20 +161,25 @@
         def _():
             pltpu.make_async_copy(tok, held.at[0], recv.at[held_sem]).start()
 
-        @pl.when(jnp.logical_not(own))
+        @pl.when(away)
         def _():
             tok_remote().start()
+
+        leaving.append(lambda away=away, copy=tok_remote: pl.when(away)(lambda: copy().wait_send()))
 
     W = [s[f"W{f}"] for f in range(NF)]
     w_gather = []
     for f in range(NF):
         for k, at in tiles_of(f):
-            if k < 3:
-                W[f][0, :, at:at + 128] = gw[:, 128 * k:128 * k + 128]
-                W[f][0, :, at + 128:at + 256] = uw[:, 128 * k:128 * k + 128]
-            else:
-                W[f][0, :, at:at + 128] = jnp.concatenate([gw[:, 384:448], uw[:, 384:448]], axis=1)
-        w_gather.append(gather_start(W[f], "x", 128))
+            n = tile_width(k) // 2
+            W[f][0, at:at + n] = gw[128 * k:128 * k + n]
+            W[f][0, at + n:at + 2 * n] = uw[128 * k:128 * k + n]
+        w_gather.append(gather_start(W[f], "x", WIDTH[f] // 2))
+    cot = s["cot"]
+    cot[...] = cot_t[...].T
+
+    def rows(f):
+        return jnp.concatenate([W[f][j] for j in range(4)], axis=1)
 
     column = (z // 2 - a + 4) % 4
     z_sem = take(4 * NT)
@@ -200,6 +206,14 @@
             for k in (1, 7, 2, 6, 3, 5, 4):
                 z_copy(h, k).start()
 
+    @functools.partial(leaving.append)
+    def _():
+        @pl.when(is_sink)
+        def _():
+            for h in range(NT):
+                for k in range(1, 8):
+                    z_copy(h, k).wait_send()
+
     def x_relay(h):
         copies = []
         for j in range(4):
@@ -214,7 +228,7 @@
 
     def project(h, f):
         x = X[h].reshape(4 * TB, 1024)
-        out = jnp.dot(x, W[f][...].reshape(1024, WIDTH[f]), preferred_element_type=f32)
+        out = lax.dot_general(x, rows(f), (((1,), (1,)), ((), ())), preferred_element_type=f32)
         out = out.reshape(4, TB, WIDTH[f])
         s[f"own{f}"][h] = out[0]
         part, keep = s[f"part{f}"].at[h], s[f"keep{f}"].at[h]
@@ -236,16 +250,16 @@
     def gate(h, f):
         reduce_finish(pre_reduce[h, f])
         pre = s[f"own{f}"][h] + s[f"finl{f}"][h].astype(f32) + s[f"finr{f}"][h].astype(f32)
-        rows = slice(h * TB, h * TB + TB)
+        mine = slice(h * TB, h * TB + TB)
         G = s[f"G{f}"]
         for k, at in tiles_of(f):
             if k < 3:
-                ct = cot[rows, 128 * k:128 * k + 128].astype(f32)
+                ct = cot[mine, 128 * k:128 * k + 128].astype(f32)
                 gg, ug = pointwise(pre[:, at:at + 128], pre[:, at + 128:at + 256], ct)
                 G[h, 0, :, at:at + 128] = gg.astype(bf16)
                 G[h, 0, :, at + 128:at + 256] = ug.astype(bf16)
             else:
-                ct = cot[rows, 384:448].astype(f32)
+                ct = cot[mine, 384:448].astype(f32)
                 ct = jnp.concatenate([ct, ct], axis=1)
                 both = pre[:, at:at + 128]
                 gg, ug = pointwise(both, pltpu.roll(both, 64, 1), ct)
@@ -258,15 +272,13 @@
     def input_grad(h, f):
         gather_finish(g_gather[h, f])
         g = s[f"G{f}"][h].reshape(4 * TB, WIDTH[f])
-        out = lax.dot_general(
-            g, W[f][...].reshape(1024, WIDTH[f]), (((1,), (1,)), ((), ())),
-            preferred_element_type=f32,
-        )
+        out = jnp.dot(g, rows(f), preferred_element_type=f32)
         for k in range(8):
             if f == 0:
                 acc[h, k] = out[:, 128 * k:128 * k + 128]
             else:
                 acc[h, k] += out[:, 128 * k:128 * k + 128]
+        s[f"GT{f}"][:, 4 * TB * h:4 * TB * h + 4 * TB] = g.T
 
     core_recv, sink_send, sink_recv = (s[n] for n in ("cr", "zs", "zr"))
     core_copies = {}
@@ -304,6 +316,8 @@
             @pl.when(zj != z)
             def _():
                 remote.start()
+
+            leaving.append(lambda zj=zj, copy=remote: pl.when(zj != z)(lambda: copy.wait_send()))
 
     last_send, last_recv = s["ls"], s["lr"]
     out_sem = take(2 * NT)
@@ -342,6 +356,17 @@
                     def _():
                         out_copy(h, 0).start()
 
+        @functools.partial(leaving.append)
+        def _():
+            @pl.when(is_sink)
+            def _():
+                for r in range(1, 4):
+                    out_copy(h, r).wait_send()
+
+                @pl.when(w != b % 2)
+                def _():
+                    out_copy(h, 0).wait_send()
+
     def dx_finish(h):
         for ww in range(2):
             pltpu.make_async_copy(
@@ -350,36 +375,32 @@
         dx_out[h * TB:h * TB + TB] = (last_recv[h, 0] + last_recv[h, 1]).astype(bf16)
 
     def weight_grad(f):
-        g = s[f"G{f}"][...].reshape(512, WIDTH[f])
+        g, n = s[f"GT{f}"][...], WIDTH[f] // 2
+        part, keep = s[f"wp{f}"], s[f"wk{f}"]
         for j in (2, 1, 3, 0):
             x = X[:, :, :, 256 * j:256 * j + 256].reshape(512, 256)
-            out = lax.dot_general(x, g, (((0,), (0,)), ((), ())), preferred_element_type=f32)
+            out = jnp.dot(g, x, preferred_element_type=f32)
             if j == 2:
-                s[f"wp{f}"][1] = out.astype(bf16)
+                part[1] = out.astype(bf16)
             elif j == 1:
-                s[f"wp{f}"][0, 128:] = out[128:].astype(bf16)
-                s[f"wk{f}"][0] = out[:128]
+                part[0, n:] = out[n:].astype(bf16)
+                keep[0] = out[:n]
             elif j == 3:
-                s[f"wp{f}"][2, :128] = out[:128].astype(bf16)
-                s[f"wk{f}"][1] = out[128:]
+                part[2, :n] = out[:n].astype(bf16)
+                keep[1] = out[n:]
+                w_reduce[f] = reduce_start(
+                    part, keep, s[f"wml{f}"], s[f"wmr{f}"], s[f"wfl{f}"], s[f"wfr{f}"], "x", n
+                )
             else:
                 s[f"wo{f}"][...] = out
-            if j == 3:
-                w_reduce[f] = reduce_start(
-                    s[f"wp{f}"], s[f"wk{f}"], s[f"wml{f}"], s[f"wmr{f}"], s[f"wfl{f}"], s[f"wfr{f}"], "x", 128
-                )
 
     def weight_finish(f):
         reduce_finish(w_reduce[f])
         total = s[f"wo{f}"][...] + s[f"wfl{f}"][...].astype(f32) + s[f"wfr{f}"][...].astype(f32)
         for k, at in tiles_of(f):
-            if k < 3:
-                gg_out[:, 128 * k:128 * k + 128] = total[:, at:at + 128]
-                ug_out[:, 128 * k:128 * k + 128] = total[:, at + 128:at + 256]
-            else:
-                both = total[:, at:at + 128]
-                gg_out[:, 384:448] = both[:, :64]
-                ug_out[:, 384:448] = pltpu.roll(both, 64, 1)[:, :64]
+            n = tile_width(k) // 2
+            gg_out[128 * k:128 * k + n] = total[at:at + n]
+            ug_out[128 * k:128 * k + n] = total[at + n:at + 2 * n]
 
     def ready(copies):
         for copy in copies:
@@ -428,41 +449,14 @@
     dx_finish(1)
     weight_finish(1)
 
-    for copy in unsent:
-        copy.wait_send()
-    for wd in range(2):
-        @pl.when(jnp.logical_not((home == b) & (w == wd)))
-        def _():
-            pltpu.make_async_remote_copy(
-                src_ref=tok, dst_ref=held.at[slot], send_sem=send.at[tok_sem + wd],
-                recv_sem=recv.at[held_sem + slot], device_id=dev(y=home, ww=wd),
-                device_id_type=MESH,
-            ).wait_send()
-
-    for h in range(NT):
-        for j in range(4):
-            zj, remote = sink_copy(h, j)
-
-            @pl.when(zj != z)
-            def _():
-                remote.wait_send()
-
-    @pl.when(is_sink)
-    def _():
-        for h in range(NT):
-            for k in range(1, 8):
-                z_copy(h, k).wait_send()
-            for r in range(1, 4):
-                out_copy(h, r).wait_send()
-
-            @pl.when(w != b % 2)
-            def _():
-                out_copy(h, 0).wait_send()
+    for wait in leaving:
+        wait()
 
 
 def scratch_shapes():
     V = pltpu.VMEM
     shapes = {
+        "cot": V((128, 448), bf16),
         "held": V((4, 128, 128), bf16),
         "X": V((NT, 4, TB, 1024), bf16),
         "acc": V((NT, 8, 4 * TB, 128), f32),
@@ -474,8 +468,9 @@
     }
     for f in range(NF):
         n = WIDTH[f]
-        shapes[f"W{f}"] = V((4, 256, n), bf16)
+        shapes[f"W{f}"] = V((4, n, 256), bf16)
         shapes[f"G{f}"] = V((NT, 4, TB, n), bf16)
+        shapes[f"GT{f}"] = V((n, 512), bf16)
         shapes[f"own{f}"] = V((NT, TB, n), f32)
         shapes[f"part{f}"] = V((NT, 3, TB, n), bf16)
         shapes[f"keep{f}"] = V((NT, 2, H, n), f32)
@@ -483,13 +478,13 @@
         shapes[f"midr{f}"] = V((NT, H, n), bf16)
         shapes[f"finl{f}"] = V((NT, TB, n), bf16)
         shapes[f"finr{f}"] = V((NT, TB, n), bf16)
-        shapes[f"wo{f}"] = V((256, n), f32)
-        shapes[f"wp{f}"] = V((3, 256, n), bf16)
-        shapes[f"wk{f}"] = V((2, 128, n), f32)
-        shapes[f"wml{f}"] = V((128, n), bf16)
-        shapes[f"wmr{f}"] = V((128, n), bf16)
-        shapes[f"wfl{f}"] = V((256, n), bf16)
-        shapes[f"wfr{f}"] = V((256, n), bf16)
+        shapes[f"wo{f}"] = V((n, 256), f32)
+        shapes[f"wp{f}"] = V((3, n, 256), bf16)
+        shapes[f"wk{f}"] = V((2, n // 2, 256), f32)
+        shapes[f"wml{f}"] = V((n // 2, 256), bf16)
+        shapes[f"wmr{f}"] = V((n // 2, 256), bf16)
+        shapes[f"wfl{f}"] = V((n, 256), bf16)
+        shapes[f"wfr{f}"] = V((n, 256), bf16)
     shapes["send"] = pltpu.SemaphoreType.DMA((SEMS,))
     shapes["recv"] = pltpu.SemaphoreType.DMA((SEMS,))
     return shapes
@@ -504,14 +499,14 @@
         kernel,
         out_shape=(
             jax.ShapeDtypeStruct((128, 128), bf16),
-            jax.ShapeDtypeStruct((256, 448), f32),
-            jax.ShapeDtypeStruct((256, 448), f32),
+            jax.ShapeDtypeStruct((448, 256), f32),
+            jax.ShapeDtypeStruct((448, 256), f32),
         ),
         in_specs=[vmem] * 4,
         out_specs=(vmem,) * 3,
         scratch_shapes=list(SCRATCH.values()),
         compiler_params=pltpu.CompilerParams(
-            collective_id=0, has_side_effects=True, vmem_limit_bytes=48 << 20
+            collective_id=0, has_side_effects=True, vmem_limit_bytes=62 << 20
         ),
         cost_estimate=pl.CostEstimate(
             flops=2_818_572_288, bytes_accessed=2_000_000, transcendentals=57344
@@ -520,20 +515,11 @@
 
 
 def shards(tokens, cotangent, gate_weight, up_weight, gate_first, up_first, gate_second, up_second):
-    input_grad, gate_wgrad, up_wgrad = gradients(tokens, cotangent, gate_weight, up_weight)
-    gate_new, gate_first_new, gate_second_new = adam_update(
-        gate_weight, gate_first, gate_second, gate_wgrad
-    )
-    up_new, up_first_new, up_second_new = adam_update(up_weight, up_first, up_second, up_wgrad)
-    return (
-        input_grad,
-        gate_new,
-        up_new,
-        gate_first_new,
-        up_first_new,
-        gate_second_new,
-        up_second_new,
-    )
+    gate_weight, up_weight = gate_weight.T, up_weight.T
+    input_grad, gate_wgrad, up_wgrad = gradients(tokens, cotangent.T, gate_weight, up_weight)
+    gate = adam_update(gate_weight, gate_first.T, gate_second.T, gate_wgrad)
+    up = adam_update(up_weight, up_first.T, up_second.T, up_wgrad)
+    return input_grad, *(new.T for pair in zip(gate, up) for new in pair)
 
 
 def solution(mesh):

time: 111 us -> 100 us (0.901)
  local copies, waits for them, and re-layouts: 12.9 us -> 0.64 us
    unnamed x28 -> x15, local copies, waits for them, and re-layouts: 12.9 us -> 0.64 us
    transpose x0 -> x1, other arithmetic: none -> 2.97 us  [shards(): return (input_grad, *(new.T for pair in zip(gate, up) for new in pair))]
    convert_element_type x1 -> x0, other arithmetic: 2.65 us -> none  [adam_update(): second_new.astype(jnp.bfloat16)]
    pallas_call x1, Pallas kernels: 94.8 us -> 95.9 us  [gradients(): pl.pallas_call(kernel, out_shape=(jax.ShapeDtypeStruct((128, 128), bf16),...]
where the time goes in v2:
time: 100 us
  Pallas kernels  95.9 us (96%)
  other arithmetic  2.97 us (3%)
    pallas_call x1, Pallas kernels, gradients(): pl.pallas_call(kernel, out_shape=(jax.ShapeDtypeStruct((128, 128), bf16),...  95.9 us
    transpose x1, other arithmetic, shards(): return (input_grad, *(new.T for pair in zip(gate, up) for new in pair))  2.97 us

profile of v2, /device:TPU:1, one launch (start us, length us, event | category | flops | bytes accessed | tf_op | source)
XLA Modules:
  0.0 100.3 jit_solution(13048910526305461224)
XLA Ops:
  0.6 0.0 copy-start
  0.6 0.0 copy-start.1
  0.7 0.0 copy-start.2
  0.7 0.0 copy-start.3
  0.7 0.0 copy-start.4
  0.7 0.0 copy-start.5
  0.7 95.9 %shard_map.135 = (bf16[128,128]{1,0:T(8,128)(2,1)}, f32[448,256]{1,0:T(8,128)}, f32[448,256]{1,0:T(8,128)}) custom-call(bf16[128,128]{1,0:T(8,128)(2,1)} %tok.1, bf16[448,128]{1,0:T(8,128)(2,1)} %bitcast.59, bf16[448,256]{1,0:T(8,128)(2,1)} %bitcast.57, bf16[448,256]{1,0:T(8,128)(2,1)} %bitcast.58), custom_call_target="tpu_custom_call" | custom-call | flops 2818572288 | bytes 2000000 | tf_op jit(solution)/shard_map/pallas_call | solution.py:498
  96.6 0.0 copy-done
  96.7 0.0 copy-done.1
  96.7 0.0 copy-done.2
  96.7 0.0 copy-done.3
  96.7 0.0 copy-done.4
  96.7 0.0 copy-done.5
  96.7 0.0 copy-start.6
  96.7 3.0 %fusion.6 = (bf16[256,448]{0,1:T(8,128)(2,1)}, bf16[256,448]{0,1:T(8,128)(2,1)}, bf16[256,448]{0,1:T(8,128)(2,1)}, bf16[256,448]{0,1:T(8,128)(2,1)}, bf16[256,448]{0,1:T(8,128)(2,1)}, /*index=5*/bf16[256,448]{0,1:T(8,128)(2,1)}) fusion(f32[448,256]{1,0:T(8,128)} %get-tuple-element.11, bf16[256,448]{0,1:T(8,128)(2,1)S(1)} %copy-done.2, ...), kind=kLoop, calls=%fused_computation.12 | loop fusion | flops 4128768 | bytes 3670016 | tf_op jit(solution)/shard_map/transpose | solution.py:522
  99.7 0.0 copy-done.6
  99.7 0.6 copy.16
Async XLA Ops:
  0.6 96.0 %copy-start = (bf16[256,448]{0,1:T(8,128)(2,1)S(1)}, bf16[256,448]{0,1:T(8,128)(2,1)}, u32[]{:S(2)}) copy-start(bf16[256,448]{0,1:T(8,128)(2,1)} %param.10) | copy-start | bytes 688132
  0.6 96.0 %copy-start.1 = (bf16[256,448]{0,1:T(8,128)(2,1)S(1)}, bf16[256,448]{0,1:T(8,128)(2,1)}, u32[]{:S(2)}) copy-start(bf16[256,448]{0,1:T(8,128)(2,1)} %param.11) | copy-start | bytes 688132
  0.7 96.0 %copy-start.2 = (bf16[256,448]{0,1:T(8,128)(2,1)S(1)}, bf16[256,448]{0,1:T(8,128)(2,1)}, u32[]{:S(2)}) copy-start(bf16[256,448]{0,1:T(8,128)(2,1)} %param.14) | copy-start | bytes 688132
  0.7 96.0 %copy-start.3 = (bf16[256,448]{0,1:T(8,128)(2,1)S(1)}, bf16[256,448]{0,1:T(8,128)(2,1)}, u32[]{:S(2)}) copy-start(bf16[256,448]{0,1:T(8,128)(2,1)} %param.12) | copy-start | bytes 688132
  0.7 96.0 %copy-start.4 = (bf16[256,448]{0,1:T(8,128)(2,1)S(1)}, bf16[256,448]{0,1:T(8,128)(2,1)}, u32[]{:S(2)}) copy-start(bf16[256,448]{0,1:T(8,128)(2,1)} %param.13) | copy-start | bytes 688132
  0.7 96.0 %copy-start.5 = (bf16[256,448]{0,1:T(8,128)(2,1)S(1)}, bf16[256,448]{0,1:T(8,128)(2,1)}, u32[]{:S(2)}) copy-start(bf16[256,448]{0,1:T(8,128)(2,1)} %param.15) | copy-start | bytes 688132
  96.7 3.0 %copy-start.6 = (bf16[128,128]{1,0:T(8,128)(2,1)S(1)}, bf16[128,128]{1,0:T(8,128)(2,1)}, u32[]{:S(2)}) copy-start(bf16[128,128]{1,0:T(8,128)(2,1)} %get-tuple-element.29) | copy-start | bytes 98308

commit v3 on v2

--- a/solution.py
+++ b/solution.py
@@ -133,6 +133,22 @@
         for copy in g[10:]:
             copy.wait_recv()
 
+    W = [s[f"W{f}"] for f in range(NF)]
+    loads = []
+    for f in range(NF):
+        copies = []
+        for k, at in tiles_of(f):
+            n = tile_width(k) // 2
+            for ref, to in ((gw, at), (uw, at + n)):
+                copy = pltpu.make_async_copy(
+                    ref.at[pl.ds(128 * k, n)], W[f].at[0, pl.ds(to, n)], recv.at[take()]
+                )
+                copy.start()
+                copies.append(copy)
+        loads.append(copies)
+    loads.append(pltpu.make_async_copy(cot_t, s["cot_t"], recv.at[take()]))
+    loads[NF].start()
+
     peers = [right["x"], left["x"], partner]
     peers += [dev(zz=(z + k) % 8) for k in range(1, 8)]
     peers += [dev(y=(b + k) % 4, ww=w) for k in range(1, 4)]
@@ -167,32 +183,65 @@
 
         leaving.append(lambda away=away, copy=tok_remote: pl.when(away)(lambda: copy().wait_send()))
 
-    W = [s[f"W{f}"] for f in range(NF)]
     w_gather = []
     for f in range(NF):
-        for k, at in tiles_of(f):
-            n = tile_width(k) // 2
-            W[f][0, at:at + n] = gw[128 * k:128 * k + n]
-            W[f][0, at + n:at + 2 * n] = uw[128 * k:128 * k + n]
+        for copy in loads[f]:
+            copy.wait()
         w_gather.append(gather_start(W[f], "x", WIDTH[f] // 2))
     cot = s["cot"]
-    cot[...] = cot_t[...].T
+    loads[NF].wait()
+    cot[...] = s["cot_t"][...].T
 
     def rows(f):
         return jnp.concatenate([W[f][j] for j in range(4)], axis=1)
 
-    column = (z // 2 - a + 4) % 4
-    z_sem = take(4 * NT)
-    z_send = take(7 * NT)
+    def column_of(dz):
+        return ((z + dz + 8) % 8 // 2 - a + 4) % 4
+
+    column = column_of(0)
+    z_sem, far_sem, core_sem = take(4 * NT), take(2 * NT), take(4 * NT)
+    z_send, pass_send, core_send = take(4 * NT), take(4 * NT), take(4 * NT)
+    STEPS = (2, -2, 1, -1)
 
     def z_dst(h, j):
         return X.at[h, :, :, pl.ds(pl.multiple_of((2 * j + c) * 128, 128), 128)]
 
-    def z_copy(h, k):
+    def z_half(h, j, half):
+        return X.at[h, pl.ds(2 * half, 2), :, pl.ds(pl.multiple_of((2 * j + c) * 128, 128), 128)]
+
+    def z_copy(h, q):
         return pltpu.make_async_remote_copy(
             src_ref=held.at[:, pl.ds(h * TB, TB)], dst_ref=z_dst(h, column),
-            send_sem=send.at[z_send + h * 7 + k - 1], recv_sem=recv.at[z_sem + 4 * h + column],
-            device_id=dev(zz=(z + k) % 8), device_id_type=MESH,
+            send_sem=send.at[z_send + 4 * h + q], recv_sem=recv.at[z_sem + 4 * h + column],
+            device_id=dev(zz=(z + STEPS[q] + 8) % 8), device_id_type=MESH,
+        )
+
+    def pass_copies(h, side):
+        j = column_of(2 * side)
+        q = pass_send + 4 * h + side + 1
+        half = (side + 1) // 2
+        return [
+            pltpu.make_async_remote_copy(
+                src_ref=z_dst(h, j), dst_ref=z_dst(h, j),
+                send_sem=send.at[q], recv_sem=recv.at[z_sem + 4 * h + j],
+                device_id=dev(zz=(z - side + 8) % 8), device_id_type=MESH,
+            ),
+            pltpu.make_async_remote_copy(
+                src_ref=z_half(h, j, half), dst_ref=z_half(h, j, half),
+                send_sem=send.at[q + 1], recv_sem=recv.at[far_sem + 2 * h + half],
+                device_id=dev(zz=(z - 2 * side + 8) % 8), device_id_type=MESH,
+            ),
+        ]
+
+    def z_wait(h, j):
+        pltpu.make_async_copy(
+            held.at[:, pl.ds(h * TB, TB)], z_dst(h, j), recv.at[z_sem + 4 * h + j]
+        ).wait()
+
+    def core_copy(h, q, j):
+        return pltpu.make_async_remote_copy(
+            src_ref=z_dst(h, j), dst_ref=z_dst(h, j), send_sem=send.at[core_send + 4 * h + q],
+            recv_sem=recv.at[core_sem + 4 * h + j], device_id=partner, device_id_type=MESH,
         )
 
     @pl.when(is_sink)
@@ -200,28 +249,64 @@
         for r in range(4):
             pltpu.make_async_copy(tok, held.at[r], recv.at[held_sem + r]).wait()
         for h in range(NT):
+            for q in range(4):
+                z_copy(h, q).start()
             pltpu.make_async_copy(
                 held.at[:, pl.ds(h * TB, TB)], z_dst(h, column), recv.at[z_sem + 4 * h + column]
             ).start()
-            for k in (1, 7, 2, 6, 3, 5, 4):
-                z_copy(h, k).start()
+
+    def x_near(h):
+        @pl.when(is_sink)
+        def _():
+            for q, side in enumerate((-1, 1)):
+                z_wait(h, column_of(2 * side))
+                for copy in pass_copies(h, side):
+                    copy.start()
+                core_copy(h, q, column_of(2 * side)).start()
+            z_wait(h, column)
+            core_copy(h, 2, column).start()
+
+        @pl.when(jnp.logical_not(is_sink))
+        def _():
+            for q, side in enumerate((-1, 1)):
+                z_wait(h, column_of(side))
+                core_copy(h, q, column_of(side)).start()
+
+    def x_far(h):
+        @pl.when(is_sink)
+        def _():
+            j = column_of(4)
+            for half in range(2):
+                pltpu.make_async_copy(
+                    held.at[pl.ds(0, 2), pl.ds(h * TB, TB)], z_half(h, j, half),
+                    recv.at[far_sem + 2 * h + half],
+                ).wait()
+            core_copy(h, 3, j).start()
+
+        @pl.when(jnp.logical_not(is_sink))
+        def _():
+            for q, side in enumerate((-3, 3)):
+                z_wait(h, column_of(side))
+                core_copy(h, 2 + q, column_of(side)).start()
+
+    def x_ready(h):
+        for j in range(4):
+            core_copy(h, j, j).wait_recv()
 
     @functools.partial(leaving.append)
     def _():
+        for h in range(NT):
+            for q in range(4):
+                core_copy(h, q, 0).wait_send()
+
         @pl.when(is_sink)
         def _():
             for h in range(NT):
-                for k in range(1, 8):
-                    z_copy(h, k).wait_send()
-
-    def x_relay(h):
-        copies = []
-        for j in range(4):
-            pltpu.make_async_copy(
-                held.at[:, pl.ds(h * TB, TB)], z_dst(h, j), recv.at[z_sem + 4 * h + j]
-            ).wait()
-            copies.append(put(z_dst(h, j), z_dst(h, j), partner))
-        return copies
+                for q in range(4):
+                    z_copy(h, q).wait_send()
+                for side in (-1, 1):
+                    for copy in pass_copies(h, side):
+                        copy.wait_send()
 
     units = [(h, f) for h in range(NT) for f in range(NF)]
     pre_reduce, g_gather, w_reduce = {}, {}, {}
@@ -402,22 +487,20 @@
             gg_out[128 * k:128 * k + n] = total[at:at + n]
             ug_out[128 * k:128 * k + n] = total[at + n:at + 2 * n]
 
-    def ready(copies):
-        for copy in copies:
-            copy.wait_recv()
-
     gather_relay(w_gather[0])
-    x0 = x_relay(0)
+    x_near(0)
+    x_far(0)
+    x_near(1)
     gather_relay(w_gather[1])
     gather_finish(w_gather[0])
-    ready(x0)
+    x_ready(0)
     project(0, 0)
     gather_finish(w_gather[1])
     project(0, 1)
+    x_far(1)
     reduce_relay(pre_reduce[0, 0])
     reduce_relay(pre_reduce[0, 1])
-    x1 = x_relay(1)
-    ready(x1)
+    x_ready(1)
     project(1, 0)
     project(1, 1)
     gate(0, 0)
@@ -457,6 +540,7 @@
     V = pltpu.VMEM
     shapes = {
         "cot": V((128, 448), bf16),
+        "cot_t": V((448, 128), bf16),
         "held": V((4, 128, 128), bf16),
         "X": V((NT, 4, TB, 1024), bf16),
         "acc": V((NT, 8, 4 * TB, 128), f32),
@@ -502,7 +586,7 @@
             jax.ShapeDtypeStruct((448, 256), f32),
             jax.ShapeDtypeStruct((448, 256), f32),
         ),
-        in_specs=[vmem] * 4,
+        in_specs=[pl.BlockSpec(memory_space=pltpu.HBM)] * 4,
         out_specs=(vmem,) * 3,
         scratch_shapes=list(SCRATCH.values()),
         compiler_params=pltpu.CompilerParams(

time: 100 us -> 99.1 us (level)
  the two profiles are of different devices: /device:TPU:1 before, /device:TPU:8 now
where the time goes in v3:
time: 99.1 us; the launch traced here: 98.9 us
  Pallas kernels  94.5 us (95%)
  other arithmetic  2.97 us (3%)
    pallas_call x1, Pallas kernels, gradients(): pl.pallas_call(kernel, out_shape=(jax.ShapeDtypeStruct((128, 128), bf16),...  94.5 us
    transpose x1, other arithmetic, shards(): return (input_grad, *(new.T for pair in zip(gate, up) for new in pair))  2.97 us

profile of v3, /device:TPU:8, one launch (start us, length us, event | category | flops | bytes accessed | tf_op | source)
XLA Modules:
  0.0 98.9 jit_solution(18414754294084156010)
XLA Ops:
  0.6 0.0 copy-start
  0.6 0.0 copy-start.1
  0.7 0.0 copy-start.2
  0.7 0.0 copy-start.3
  0.7 0.0 copy-start.4
  0.7 0.0 copy-start.5
  0.7 94.5 %shard_map.135 = (bf16[128,128]{1,0:T(8,128)(2,1)}, f32[448,256]{1,0:T(8,128)}, f32[448,256]{1,0:T(8,128)}) custom-call(bf16[128,128]{1,0:T(8,128)(2,1)} %tok.1, bf16[448,128]{1,0:T(8,128)(2,1)} %bitcast.59, bf16[448,256]{1,0:T(8,128)(2,1)} %bitcast.57, bf16[448,256]{1,0:T(8,128)(2,1)} %bitcast.58), custom_call_target="tpu_custom_call" | custom-call | flops 2818572288 | bytes 2000000 | tf_op jit(solution)/shard_map/pallas_call | solution.py:582
  95.2 0.0 copy-done
  95.2 0.0 copy-done.1
  95.2 0.0 copy-done.2
  95.2 0.0 copy-done.3
  95.2 0.0 copy-done.4
  95.2 0.0 copy-done.5
  95.3 0.0 copy-start.6
  95.3 3.0 %fusion.6 = (bf16[256,448]{0,1:T(8,128)(2,1)}, bf16[256,448]{0,1:T(8,128)(2,1)}, bf16[256,448]{0,1:T(8,128)(2,1)}, bf16[256,448]{0,1:T(8,128)(2,1)}, bf16[256,448]{0,1:T(8,128)(2,1)}, /*index=5*/bf16[256,448]{0,1:T(8,128)(2,1)}) fusion(f32[448,256]{1,0:T(8,128)} %get-tuple-element.11, bf16[256,448]{0,1:T(8,128)(2,1)S(1)} %copy-done.2, ...), kind=kLoop, calls=%fused_computation.12 | loop fusion | flops 4128768 | bytes 3670016 | tf_op jit(solution)/shard_map/transpose | solution.py:606
  98.2 0.0 copy-done.6
  98.2 0.6 copy.16
Async XLA Ops:
  0.6 94.6 %copy-start = (bf16[256,448]{0,1:T(8,128)(2,1)S(1)}, bf16[256,448]{0,1:T(8,128)(2,1)}, u32[]{:S(2)}) copy-start(bf16[256,448]{0,1:T(8,128)(2,1)} %param.10) | copy-start | bytes 688132
  0.6 94.6 %copy-start.1 = (bf16[256,448]{0,1:T(8,128)(2,1)S(1)}, bf16[256,448]{0,1:T(8,128)(2,1)}, u32[]{:S(2)}) copy-start(bf16[256,448]{0,1:T(8,128)(2,1)} %param.11) | copy-start | bytes 688132
  0.7 94.6 %copy-start.2 = (bf16[256,448]{0,1:T(8,128)(2,1)S(1)}, bf16[256,448]{0,1:T(8,128)(2,1)}, u32[]{:S(2)}) copy-start(bf16[256,448]{0,1:T(8,128)(2,1)} %param.14) | copy-start | bytes 688132
  0.7 94.6 %copy-start.3 = (bf16[256,448]{0,1:T(8,128)(2,1)S(1)}, bf16[256,448]{0,1:T(8,128)(2,1)}, u32[]{:S(2)}) copy-start(bf16[256,448]{0,1:T(8,128)(2,1)} %param.12) | copy-start | bytes 688132
  0.7 94.6 %copy-start.4 = (bf16[256,448]{0,1:T(8,128)(2,1)S(1)}, bf16[256,448]{0,1:T(8,128)(2,1)}, u32[]{:S(2)}) copy-start(bf16[256,448]{0,1:T(8,128)(2,1)} %param.13) | copy-start | bytes 688132
  0.7 94.6 %copy-start.5 = (bf16[256,448]{0,1:T(8,128)(2,1)S(1)}, bf16[256,448]{0,1:T(8,128)(2,1)}, u32[]{:S(2)}) copy-start(bf16[256,448]{0,1:T(8,128)(2,1)} %param.15) | copy-start | bytes 688132
  95.3 3.0 %copy-start.6 = (bf16[128,128]{1,0:T(8,128)(2,1)S(1)}, bf16[128,128]{1,0:T(8,128)(2,1)}, u32[]{:S(2)}) copy-start(bf16[128,128]{1,0:T(8,128)(2,1)} %get-tuple-element.29) | copy-start | bytes 98308
